TPU v7x, 1024 devices: a whole 4x4x32 slice. The times are simulated.
1024 devices in a mesh: replica: 32 (over x, y, core), mp: 32 (over z).
Axes of the slice: x: 4, y: 4, z: 32, core: 2. Of those that a mesh axis runs over, the one named last changes fastest.
Arguments:
- table: float32 [65536, 128], P('mp'), may hold values from -3 to 3
- accum: float32 [65536, 128], P('mp'), may hold values from 0.01 to 4
- request_ids: int32 [1024, 32, 128], P(('replica', 'mp')), may hold values from 0 to 2047
- send_counts: int32 [1024, 32], P(('replica', 'mp')), may hold values from 1 to 128, as said below
- entry_slots: int32 [262144, 16], P(('replica', 'mp')), may hold values from 0 to 4095
- entry_weights: bfloat16 [262144, 16], P(('replica', 'mp')), may hold values from 0.25 to 2
- pooled_grad: bfloat16 [262144, 128], P(('replica', 'mp')), may hold values from -6 to 6
Outputs:
- pooled: bfloat16 [262144, 128], P(('replica', 'mp'))
- new_table: float32 [65536, 128], P('mp')
- new_accum: float32 [65536, 128], P('mp')
Inputs may be any that keep to these rules, and one draw needn't show every extreme that they name: `send_counts`: every device has one to 128 live slots for each owner; in every draw one owner has 128 live slots from every device.
All inputs are finite; a program needn't handle non-finite values.
Results may differ from a plain program's by a relative error of at most 0.0049.
Values may be sent and summed in bfloat16 or wider, within the bound.
A program may use at most 64 MiB of HBM per device.

v0:
```python
import jax
import jax.numpy as jnp
from jax import lax
from jax.sharding import PartitionSpec as P

learn_rate = 0.5


def adagrad(table, accum, grad):
    fresh = accum + grad * grad
    return (table - learn_rate * grad / jnp.sqrt(fresh), fresh)


def per_device(table, accum, request_ids, send_counts, entry_slots, entry_weights, pooled_grad):
    peers = lax.axis_size("mp")
    asked = request_ids.reshape(peers, -1)
    capacity = asked.shape[1]
    width = table.shape[1]
    slot_count = peers * capacity
    received = lax.all_to_all(asked, "mp", split_axis=0, concat_axis=0, tiled=True)
    looked = jnp.take(table, received, axis=0).astype(jnp.bfloat16)
    arrived = lax.all_to_all(looked, "mp", split_axis=0, concat_axis=0, tiled=True)
    rows, received = (arrived, received)
    flat_rows = rows.reshape(slot_count, width)
    column = lax.broadcasted_iota(jnp.int32, (peers, capacity), 1)
    live = (column < send_counts.reshape(peers, 1)).reshape(-1).astype(jnp.float32)
    samples = entry_slots.shape[0]
    bag_len = entry_slots.shape[1]
    slot_iota = lax.broadcasted_iota(jnp.int32, (samples, slot_count), 1)
    weights = entry_weights.astype(jnp.float32)

    def add_entry(index, incidence):
        slot_col = lax.dynamic_slice_in_dim(entry_slots, index, 1, 1)
        weight_col = lax.dynamic_slice_in_dim(weights, index, 1, 1)
        return incidence + jnp.where(slot_iota == slot_col, weight_col, 0.0)

    incidence = lax.fori_loop(0, bag_len, add_entry, jnp.zeros((samples, slot_count), jnp.float32))
    incidence = incidence * live[None, :]
    pooled = jnp.dot(
        incidence,
        flat_rows.astype(jnp.float32),
        precision=lax.Precision.HIGHEST,
        preferred_element_type=jnp.float32,
    ).astype(jnp.bfloat16)
    slot_grad = lax.dot_general(
        incidence,
        pooled_grad.astype(jnp.float32),
        (((0,), (0,)), ((), ())),
        precision=lax.Precision.HIGHEST,
        preferred_element_type=jnp.float32,
    )
    returned = lax.all_to_all(
        slot_grad.reshape(peers, capacity, width), "mp", split_axis=0, concat_axis=0, tiled=True
    )
    row_grad = jax.ops.segment_sum(
        returned.reshape(-1, width), received.reshape(-1), num_segments=table.shape[0]
    )
    total = lax.psum(row_grad, "replica")
    new_table, new_accum = adagrad(table, accum, total)
    return (pooled, new_table, new_accum)


def solution(mesh):
    return jax.shard_map(
        per_device,
        mesh=mesh,
        in_specs=(
            P("mp", None),
            P("mp", None),
            P(("replica", "mp"), None, None),
            P(("replica", "mp"), None),
            P(("replica", "mp"), None),
            P(("replica", "mp"), None),
            P(("replica", "mp"), None),
        ),
        out_specs=(P(("replica", "mp"), None), P("mp", None), P("mp", None)),
        check_vma=False,
    )
```

profile of v0, /device:TPU:1, one launch (start us, length us, event | category | flops | bytes accessed | tf_op | source)
XLA Modules:
  0.0 572.7 jit_solution(15078652574267271999)
XLA Ops:
  7.2 29.4 %all-to-all-start = ((s32[32,1,128]{2,1,0:T(1,128)}), s32[32,1,128]{2,1,0:T(1,128)S(1)}, u32[]{:S(2)}, u32[]{:S(2)}) async-start(s32[32,1,128]{2,1,0:T(1,128)} %bitcast.30), calls=%async_computation | async-start | bytes 32768 | tf_op jit(solution)/shard_map/all_to_all | solution.py:20
  36.6 0.7 convert_element_type.21
  37.3 90.9 %while.14 = (s32[]{:T(128)}, f32[256,4096]{1,0:T(8,128)}, s32[256,16]{0,1:T(8,128)}, f32[256,16]{0,1:T(8,128)S(1)}, s32[]{:T(128)}, /*index=5*/s32[]{:T(128)}) while((s32[]{:T(128)}, f32[256,4096]{1,0:T(8,128)}, s32[256,16]{0,1:T(8,128)}, f32[256,16]{0,1:T(8,128)S(1)}, s32[]{:T(128)}, /*index=5*/s32[]{:T(128)}) %tuple.37), condition=%wide.region_1.2_spmd.clone, body=%wide.region_0.1_spmd.clone.sunk | while | flops 4194307 | bytes 8394839 | solution.py:37
  37.3 0.7 constant_dynamic-slice_fusion.5
  38.0 2.9 select_add_fusion.2
  41.0 0.7 constant_dynamic-slice_fusion.5
  41.7 5.1 select_add_fusion.2
  46.8 0.7 constant_dynamic-slice_fusion.5
  47.5 5.1 select_add_fusion.2
  52.6 0.7 constant_dynamic-slice_fusion.5
  53.3 5.1 select_add_fusion.2
  58.4 0.7 constant_dynamic-slice_fusion.5
  59.1 5.1 select_add_fusion.2
  64.2 0.7 constant_dynamic-slice_fusion.5
  64.9 5.1 select_add_fusion.2
  70.1 0.7 constant_dynamic-slice_fusion.5
  70.8 5.1 select_add_fusion.2
  75.9 0.7 constant_dynamic-slice_fusion.5
  76.6 5.1 select_add_fusion.2
  81.7 0.7 constant_dynamic-slice_fusion.5
  82.4 5.1 select_add_fusion.2
  87.5 0.7 constant_dynamic-slice_fusion.5
  88.2 5.1 select_add_fusion.2
  93.3 0.7 constant_dynamic-slice_fusion.5
  94.0 5.1 select_add_fusion.2
  99.1 0.7 constant_dynamic-slice_fusion.5
  99.8 5.1 select_add_fusion.2
  105.0 0.7 constant_dynamic-slice_fusion.5
  105.7 5.1 select_add_fusion.2
  110.8 0.7 constant_dynamic-slice_fusion.5
  111.5 5.1 select_add_fusion.2
  116.6 0.7 constant_dynamic-slice_fusion.5
  117.3 5.1 select_add_fusion.2
  122.4 0.7 constant_dynamic-slice_fusion.5
  123.1 5.1 select_add_fusion.2
  128.2 0.1 convert_bitcast_fusion
  128.3 7.1 %fusion.2 = f32[4096,128]{1,0:T(8,128)} fusion(bf16[256,128]{1,0:T(8,128)(2,1)S(1)} %copy-done, f32[256,4096]{1,0:T(8,128)} %get-tuple-element.97, f32[4096]{0:T(1024)S(1)} %convert_bitcast_fusion), kind=kOutput, calls=%fused_computation.7 | convolution fusion | flops 1611661312 | bytes 6373376 | tf_op jit(solution)/shard_map/dot_general | solution.py:45
  135.4 21.4 %all-to-all-start.2 = ((f32[32,128,128]{2,1,0:T(8,128)}), f32[32,128,128]{2,1,0:T(8,128)}, u32[]{:S(2)}, u32[]{:S(2)}) async-start(f32[32,128,128]{2,1,0:T(8,128)} %bitcast.9), calls=%async_computation.2 | async-start | bytes 4194304 | tf_op jit(solution)/shard_map/all_to_all | solution.py:52
  156.8 11.0 %gather_fusion = bf16[4096,128]{1,0:T(8,128)(2,1)S(1)} fusion(f32[2048,128]{1,0:T(8,128)S(1)} %copy-done.1, s32[4096]{0:T(1024)S(1)} %fusion.14), kind=kCustom, calls=%fused_computation | custom fusion | bytes 2113536 | tf_op jit(solution)/shard_map/jit(_take)/gather | solution.py:21
  167.8 1.5 select_convert_fusion
  169.3 179.8 %all-to-all-done.2 = f32[32,128,128]{2,1,0:T(8,128)} async-done(((f32[32,128,128]{2,1,0:T(8,128)}), f32[32,128,128]{2,1,0:T(8,128)}, u32[]{:S(2)}, u32[]{:S(2)}) %all-to-all-start.2) | async-done | bytes 2097184 | tf_op jit(solution)/shard_map/all_to_all | solution.py:52
  349.1 10.1 %all-to-all-start.1 = ((bf16[32,128,128]{2,1,0:T(8,128)(2,1)}), bf16[32,128,128]{2,1,0:T(8,128)(2,1)S(1)}, u32[]{:S(2)}, u32[]{:S(2)}) async-start(bf16[32,128,128]{2,1,0:T(8,128)(2,1)} %select_convert_fusion), calls=%async_computation.1 | async-start | bytes 2097152 | tf_op jit(solution)/shard_map/all_to_all | solution.py:22
  359.2 0.0 all-reduce.2.cloned.1.call-start
  359.3 23.7 %scatter_custom_fusion = f32[2048,128]{1,0:T(8,128)} fusion(s32[4096]{0:T(1024)S(1)} %bitcast.27, f32[4096,128]{1,0:T(8,128)} %bitcast.10, f32[]{:T(128)} %constant.45.clone.1), kind=kCustom, calls=%fused_computation.17 | custom fusion | flops 524288 | bytes 1049088 | tf_op jit(solution)/shard_map/scatter-add | solution.py:55
  383.0 81.7 %all-to-all-done.1 = bf16[32,128,128]{2,1,0:T(8,128)(2,1)S(1)} async-done(((bf16[32,128,128]{2,1,0:T(8,128)(2,1)}), bf16[32,128,128]{2,1,0:T(8,128)(2,1)S(1)}, u32[]{:S(2)}, u32[]{:S(2)}) %all-to-all-start.1) | async-done | bytes 1048608 | tf_op jit(solution)/shard_map/all_to_all | solution.py:22
  464.7 4.9 fusion.8
  469.6 93.5 %all-reduce.2.cloned.1.call-done = f32[2048,128]{1,0:T(8,128)} async-done(((f32[2048,128]{1,0:T(8,128)}), f32[2048,128]{1,0:T(8,128)}) %all-reduce.2.cloned.1.call-update) | async-done | bytes 1048592 | tf_op jit(solution)/shard_map/psum | solution.py:58
  563.1 2.7 multiply_subtract_fusion
  (29 shorter events, 0.2 us)
Async XLA Ops:
  7.2 121.1 %copy-start = (bf16[256,128]{1,0:T(8,128)(2,1)S(1)}, bf16[256,128]{1,0:T(8,128)(2,1)}, u32[]{:S(2)}) copy-start(bf16[256,128]{1,0:T(8,128)(2,1)} %param.15) | copy-start | bytes 196612
  7.2 128.2 %all-to-all-start = ((s32[32,1,128]{2,1,0:T(1,128)}), s32[32,1,128]{2,1,0:T(1,128)S(1)}, u32[]{:S(2)}, u32[]{:S(2)}) async-start(s32[32,1,128]{2,1,0:T(1,128)} %bitcast.30), calls=%async_computation | async-start | bytes 32768 | tf_op jit(solution)/shard_map/all_to_all | solution.py:20
  37.3 90.9 %copy-start.3 = (s32[1,32]{1,0:T(1,128)S(1)}, s32[1,32]{1,0:T(1,128)}, u32[]{:S(2)}) copy-start(s32[1,32]{1,0:T(1,128)} %param.12) | copy-start | bytes 388
  128.3 28.5 %copy-start.1 = (f32[2048,128]{1,0:T(8,128)S(1)}, f32[2048,128]{1,0:T(8,128)}, u32[]{:S(2)}) copy-start(f32[2048,128]{1,0:T(8,128)} %param.9) | copy-start | bytes 3145732
  135.4 213.7 %all-to-all-start.2 = ((f32[32,128,128]{2,1,0:T(8,128)}), f32[32,128,128]{2,1,0:T(8,128)}, u32[]{:S(2)}, u32[]{:S(2)}) async-start(f32[32,128,128]{2,1,0:T(8,128)} %bitcast.9), calls=%async_computation.2 | async-start | bytes 4194304 | tf_op jit(solution)/shard_map/all_to_all | solution.py:52
  349.1 115.6 %all-to-all-start.1 = ((bf16[32,128,128]{2,1,0:T(8,128)(2,1)}), bf16[32,128,128]{2,1,0:T(8,128)(2,1)S(1)}, u32[]{:S(2)}, u32[]{:S(2)}) async-start(bf16[32,128,128]{2,1,0:T(8,128)(2,1)} %select_convert_fusion), calls=%async_computation.1 | async-start | bytes 2097152 | tf_op jit(solution)/shard_map/all_to_all | solution.py:22
  359.2 203.9 %copy-start.2 = (f32[2048,128]{1,0:T(8,128)S(1)}, f32[2048,128]{1,0:T(8,128)}, u32[]{:S(2)}) copy-start(f32[2048,128]{1,0:T(8,128)} %param.10) | copy-start | bytes 3145732
  359.2 203.9 %all-reduce.2.cloned.1.call-start = ((), (), s32[]{:S(2)}) async-start(), calls=%async_computation.3 | async-start | bytes 2097152 | tf_op jit(solution)/shard_map/psum | solution.py:58
Sparse Core Ops, SparseCore 0:
  383.2 179.9 all-reduce.1
where the time goes:
time: 574 us; the launch traced here: 573 us
  waiting for transfers between devices  355 us (62%)
  other arithmetic  108 us (19%)
  starting transfers between devices  60.9 us (11%)
  local copies, waits for them, and re-layouts  22.4 us (4%)
  between operations  14.1 us (2%)
  matrix products  12 us (2%)
    all_to_all x1, waiting for transfers between devices, per_device(): lax.all_to_all(slot_grad.reshape(peers, capacity, width), 'mp', split_axi...  180 us
    psum x1, waiting for transfers between devices, per_device(): total = lax.psum(row_grad, 'replica')  93.5 us
    all_to_all x1, waiting for transfers between devices, per_device(): lax.all_to_all(looked, 'mp', split_axis=0, concat_axis=0, tiled=True)  81.7 us
    add x16, other arithmetic, add_entry(): return incidence + jnp.where(slot_iota == slot_col, weight_col, 0.0)  79.6 us
    all_to_all x1, starting transfers between devices, per_device(): lax.all_to_all(asked, 'mp', split_axis=0, concat_axis=0, tiled=True)  29.4 us
    scatter-add x1, other arithmetic, per_device(): jax.ops.segment_sum(returned.reshape(-1, width), received.reshape(-1), nu...  23.7 us
    all_to_all x1, starting transfers between devices, per_device(): lax.all_to_all(slot_grad.reshape(peers, capacity, width), 'mp', split_axi...  21.4 us
  transfers between devices with their start and end apart: 4, of which 3 were waited for; matrix products, arithmetic and copies ran while one was open for 24% of the time, Pallas kernels for 0%

commit v1 on v0

v1 whole, which is shorter than its diff:
```python
import functools

import jax
import jax.numpy as jnp
from jax import lax
from jax.experimental import pallas as pl
from jax.experimental.pallas import tpu as pltpu
from jax.sharding import PartitionSpec as P

learn_rate = 0.5
FAR = 8
NEAR = 4
SIDE = 4
MESH = pl.DeviceIdType.MESH


def remote(src, dst, send_sem, recv_sem, r, z):
    return pltpu.make_async_remote_copy(
        src_ref=src, dst_ref=dst, send_sem=send_sem, recv_sem=recv_sem,
        device_id={"replica": r, "mp": z}, device_id_type=MESH,
    )


def place(index):
    return lax.rem(index, NEAR) * FAR + index // NEAR


class Seat:
    def __init__(self, n):
        self.n = n
        self.r, self.z = lax.axis_index("replica"), lax.axis_index("mp")
        self.x, self.y, self.c = self.r // (2 * SIDE), lax.rem(self.r // 2, SIDE), lax.rem(self.r, 2)
        self.a, self.b = self.z // NEAR, lax.rem(self.z, NEAR)
        self.twin = self.r + 1 - 2 * self.c

    def x_at(self, o):
        return lax.rem(self.x + o, SIDE)

    def y_at(self, o):
        return lax.rem(self.y + o, SIDE)

    def along_x(self, o):
        return (self.x_at(o) * SIDE + self.y) * 2 + self.c

    def along_y(self, o):
        return (self.x * SIDE + self.y_at(o)) * 2 + self.c

    def up(self, o):
        return lax.rem(self.z + o + self.n, self.n)

    def greet(self):
        barrier = pltpu.get_barrier_semaphore()

        def hello(r, z):
            pl.semaphore_signal(barrier, inc=1, device_id={"replica": r, "mp": z}, device_id_type=MESH)

        @pl.loop(1, SIDE)
        def _(o):
            hello(self.along_x(o), self.z)
            hello(self.along_y(o), self.z)

        @pl.loop(1, FAR)
        def _(o):
            hello(self.r, self.up(NEAR * o))

        hello(self.twin, self.z)
        for o in (-2, -1, 1, 2):
            hello(self.r, self.up(o))

        @pl.when(self.r != self.z)
        def _():
            hello(self.z, self.r)

        pl.semaphore_wait(barrier, 2 * (SIDE - 1) + FAR - 1 + 5 + jnp.where(self.r != self.z, 1, 0))

    def turn(self, src, dst, dst_local, sems):
        def away():
            return remote(src, dst, sems.at[0], sems.at[1], self.z, self.r)

        def here():
            return pltpu.make_async_copy(src, dst_local, sems.at[2])

        def start():
            @pl.when(self.r != self.z)
            def _():
                away().start()

            @pl.when(self.r == self.z)
            def _():
                here().start()

        def wait():
            @pl.when(self.r != self.z)
            def _():
                away().wait()

            @pl.when(self.r == self.z)
            def _():
                here().wait()

        return start, wait


def start_each(last, *copies):
    @pl.loop(1, last)
    def _(o):
        for copy in copies:
            copy(o).start()


def wait_each(last, *copies):
    @pl.loop(1, last)
    def _(o):
        for copy in copies:
            copy(o).wait()


def inward(n, piece_ref, ids_ref, grad_ref, table_out, ids_out, grad_out, ids_x, ids_y, grad_x, grad_y, grad_b,
           turn_sem, own_sem, far_send, far_recv, near_send, near_recv, id_send, id_recv, grad_send, grad_recv):
    seat = Seat(n)
    r, z, x, y, c = seat.r, seat.z, seat.x, seat.y, seat.c
    cut = grad_x.shape[3]
    low, high = pl.ds(0, cut), pl.ds(cut, cut)
    seat.greet()
    mine = table_out.at[place(z)]
    turn_start, turn_wait = seat.turn(piece_ref, table_out.at[place(r)], mine, turn_sem)
    turn_start()

    def ship(src, dst, k, to):
        return remote(src, dst, grad_send.at[k], grad_recv.at[k], to, z)

    def ship_ids(src, dst, k, to):
        return remote(src, dst, id_send.at[k], id_recv.at[k], to, z)

    def x_low(o):
        return ship(grad_ref.at[seat.x_at(o), :, :, low], grad_x.at[x], o, seat.along_x(o))

    def y_high(o):
        return ship(grad_ref.at[:, seat.y_at(o), :, high], grad_y.at[y], SIDE + o, seat.along_y(o))

    def y_low(o):
        return ship(grad_x.at[:, seat.y_at(o)], grad_b.at[y, :, :, low], 2 * SIDE + o, seat.along_y(o))

    def x_high(o):
        return ship(grad_y.at[:, seat.x_at(o)], grad_b.at[:, x, :, high], 3 * SIDE + o, seat.along_x(o))

    def x_ids(o):
        return ship_ids(ids_ref.at[seat.x_at(o)], ids_x.at[x], o, seat.along_x(o))

    def y_ids(o):
        return ship_ids(ids_x.at[:, seat.y_at(o)], ids_y.at[y], SIDE + o, seat.along_y(o))

    own = [pltpu.make_async_copy(src, dst, own_sem.at[k]) for k, (src, dst) in enumerate((
        (grad_ref.at[x, :, :, low], grad_x.at[x]),
        (grad_ref.at[:, y, :, high], grad_y.at[y]),
        (ids_ref.at[x], ids_x.at[x]),
        (grad_x.at[:, y], grad_b.at[y, :, :, low]),
        (grad_y.at[:, x], grad_b.at[:, x, :, high]),
        (ids_x.at[:, y], ids_y.at[y]),
        (grad_b.at[:, :, c], grad_out.at[c]),
        (ids_y.at[:, :, c], ids_out.at[c]),
    ))]
    start_each(SIDE, x_low, y_high, x_ids)
    for copy in own[:3]:
        copy.start()

    turn_wait()

    def far(o):
        return remote(mine, mine, far_send.at[o], far_recv.at[o], r, seat.up(NEAR * o))

    start_each(FAR, far)
    for copy in own[:3]:
        copy.wait()
    wait_each(SIDE, x_low, y_high, x_ids)
    start_each(SIDE, y_low, x_high, y_ids)
    for copy in own[3:6]:
        copy.start()
    wait_each(FAR, far)

    def near(k, first, count, o):
        block = table_out.at[pl.ds(seat.b * FAR + first, count)]
        return remote(block, block, near_send.at[k], near_recv.at[k], r, seat.up(o))

    half = FAR // 2
    nears = [near(0, 0, FAR, 1), near(1, 0, FAR, -1), near(2, 0, half, 2), near(3, half, half, -2)]
    for copy in nears:
        copy.start()
    for copy in own[3:6]:
        copy.wait()
    wait_each(SIDE, y_low, x_high, y_ids)
    twins = [ship(grad_b.at[:, :, 1 - c], grad_out.at[c], 0, seat.twin),
             ship_ids(ids_y.at[:, :, 1 - c], ids_out.at[c], 0, seat.twin)]
    for copy in twins + own[6:]:
        copy.start()
    for copy in twins + own[6:] + nears:
        copy.wait()


def outward(n, part_ref, rows_ref, rows_out, grad_out, rows_b, rows_y, rows_x, near_a, near_b, near_c, near_d,
            total, far_out, far_in, piece,
            turn_sem, own_sem, far_send, far_recv, near_send, near_recv, row_send, row_recv, fin_send, fin_recv):
    seat = Seat(n)
    r, z, x, y, c, b = seat.r, seat.z, seat.x, seat.y, seat.c, seat.b
    half = FAR // 2
    cut = rows_y.shape[3]
    low, high = pl.ds(0, cut), pl.ds(cut, cut)
    seat.greet()

    def near(k, first, count, o, dst):
        block = part_ref.at[lax.rem(b + o + NEAR, NEAR), pl.ds(first, count)]
        return remote(block, dst, near_send.at[k], near_recv.at[k], r, seat.up(o))

    nears = [near(0, 0, FAR, 1, near_a), near(1, 0, FAR, -1, near_b),
             near(2, 0, half, 2, near_c), near(3, half, half, -2, near_d)]
    for copy in nears:
        copy.start()

    def ship(src, dst, k, to):
        return remote(src, dst, row_send.at[k], row_recv.at[k], to, z)

    def y_low(o):
        return ship(rows_b.at[:, seat.y_at(o), :, low], rows_y.at[y], o, seat.along_y(o))

    def x_high(o):
        return ship(rows_b.at[:, :, seat.x_at(o), high], rows_x.at[x], SIDE + o, seat.along_x(o))

    def x_low(o):
        return ship(rows_y.at[:, :, seat.x_at(o)], rows_out.at[x, :, :, low], 2 * SIDE + o, seat.along_x(o))

    def y_high(o):
        return ship(rows_x.at[:, :, seat.y_at(o)], rows_out.at[:, y, :, high], 3 * SIDE + o, seat.along_y(o))

    own = [pltpu.make_async_copy(src, dst, own_sem.at[k]) for k, (src, dst) in enumerate((
        (rows_ref.at[c], rows_b.at[c]),
        (rows_b.at[:, y, :, low], rows_y.at[y]),
        (rows_b.at[:, :, x, high], rows_x.at[x]),
        (rows_y.at[:, :, x], rows_out.at[x, :, :, low]),
        (rows_x.at[:, :, y], rows_out.at[:, y, :, high]),
    ))]
    twin = ship(rows_ref.at[1 - c], rows_b.at[c], 0, seat.twin)
    twin.start()
    own[0].start()
    own[0].wait()
    twin.wait()
    start_each(SIDE, y_low, x_high)
    own[1].start()
    own[2].start()

    for copy in nears:
        copy.wait()
    for first, far_half in ((0, near_c), (half, near_d)):
        here = pl.ds(first, half)
        total[here] = (part_ref[b, here] + near_a[here]) + (near_b[here] + far_half[...])
    far_out[...] = total[...].astype(jnp.bfloat16)

    def far(o):
        return remote(far_out.at[lax.rem(seat.a + o, FAR)], far_in.at[o], far_send.at[o], far_recv.at[o],
                      r, seat.up(NEAR * o))

    start_each(FAR, far)
    own[1].wait()
    own[2].wait()
    wait_each(SIDE, y_low, x_high)
    start_each(SIDE, x_low, y_high)
    own[3].start()
    own[4].start()
    wait_each(FAR, far)
    far_sum = total[seat.a]
    for o in range(1, FAR):
        far_sum = far_sum + far_in[o].astype(jnp.float32)
    piece[...] = far_sum

    here = grad_out.at[x, y, c]
    afar = grad_out.at[z // (2 * SIDE), lax.rem(z // 2, SIDE), lax.rem(z, 2)]
    turn_start, turn_wait = seat.turn(piece, afar, here, turn_sem)
    turn_start()
    own[3].wait()
    own[4].wait()
    wait_each(SIDE, x_low, y_high)
    turn_wait()

    rows = piece.shape[0] // 2
    upper, lower = pl.ds(0, rows), pl.ds(rows, rows)

    def spread(ref, k, to):
        return remote(ref, ref, fin_send.at[k], fin_recv.at[k], to, z)

    def x_upper(o):
        return spread(grad_out.at[x, y, c, upper], o, seat.along_x(o))

    def y_lower(o):
        return spread(grad_out.at[x, y, c, lower], SIDE + o, seat.along_y(o))

    def y_upper(o):
        return spread(grad_out.at[:, y, c, upper], 2 * SIDE + o, seat.along_y(o))

    def x_lower(o):
        return spread(grad_out.at[x, :, c, lower], 3 * SIDE + o, seat.along_x(o))

    start_each(SIDE, x_upper, y_lower)
    wait_each(SIDE, x_upper, y_lower)
    start_each(SIDE, y_upper, x_lower)
    wait_each(SIDE, y_upper, x_lower)
    last = spread(grad_out.at[:, :, c], 0, seat.twin)
    last.start()
    last.wait()


SUB = 64


def incidence(capacity, counts_ref, slots_ref, weights_ref, cot_ref, inc_ref, grad_ref, hot):
    block, samples = inc_ref.shape
    bag = slots_ref.shape[0]
    step = pl.program_id(0)

    @pl.when(step == 0)
    def _():
        column = lax.broadcasted_iota(jnp.int32, (capacity, samples), 0)
        for entry in range(bag):
            low = lax.rem(slots_ref[entry:entry + 1, :], capacity)
            hot[entry] = jnp.where(column == low, 1.0, 0.0)

    @pl.loop(0, block // capacity)
    def _(part):
        owner = step * (block // capacity) + part
        weights = jnp.where(slots_ref[...] // capacity == owner, weights_ref[...].astype(jnp.float32), 0.0)
        for first in range(0, capacity, SUB):
            total = hot[0, first:first + SUB] * weights[0:1, :]
            for entry in range(1, bag):
                total += hot[entry, first:first + SUB] * weights[entry:entry + 1, :]
            slot = first + lax.broadcasted_iota(jnp.int32, (SUB, samples), 0)
            total = jnp.where(slot < counts_ref[owner], total, 0.0)
            here = pl.ds(pl.multiple_of(part * capacity + first, SUB), SUB)
            inc_ref[here, :] = total.astype(jnp.bfloat16)

    grad_ref[...] = jnp.dot(inc_ref[...], cot_ref[...], preferred_element_type=jnp.float32).astype(jnp.bfloat16)


def lookup_and_sum(ids_ref, grad_ref, table_ref, rows_ref, part_ref, pick, spread):
    group, _, capacity = ids_ref.shape
    half, width = table_ref.shape[0], table_ref.shape[1] // 2
    bf16 = jnp.bfloat16
    one, zero = jnp.ones((capacity, 128), bf16), jnp.zeros((capacity, 128), bf16)
    lane = lax.broadcasted_iota(jnp.int32, (capacity, 128), 1).astype(jnp.float32).astype(bf16)
    row = lax.broadcasted_iota(jnp.int32, (128, capacity), 0).astype(jnp.float32).astype(bf16)
    tops, doubled = [], []

    def split(ids):
        low = jnp.bitwise_and(ids, 127).astype(jnp.float32).astype(bf16)
        mid = jnp.bitwise_and(lax.shift_right_logical(ids, 7), half // 128 - 1).astype(jnp.float32).astype(bf16)
        return low, mid, ids >= half

    unit = 2 * half // (NEAR * FAR)

    for q in range(group):
        spot = ids_ref[q]
        spot = (lax.rem(spot // unit, NEAR) * FAR + spot // (unit * NEAR)) * unit + lax.rem(spot, unit)
        ids = jnp.broadcast_to(spot, (capacity, capacity))
        column = ids.astype(jnp.float32).T.astype(jnp.int32)
        here = slice(q * capacity, (q + 1) * capacity)
        low, mid, top = split(column)
        hot = jnp.where(lane == low, one, zero)
        for tile in range(half // 128):
            pick[here, tile * 128:(tile + 1) * 128] = jnp.where(mid == jnp.full_like(mid, tile), hot, zero)
        tops.append(top)
        cot = grad_ref[q].astype(jnp.float32)
        doubled.append(jnp.concatenate(
            [jnp.where(top, 0.0, cot).astype(bf16), jnp.where(top, cot, 0.0).astype(bf16)], axis=1))
        low, mid, _ = split(ids)
        hot = jnp.where(row == low, one, zero)
        for tile in range(half // 128):
            spread[tile * 128:(tile + 1) * 128, here] = jnp.where(mid == jnp.full_like(mid, tile), hot, zero)

    looked = jnp.dot(pick[...], table_ref[...], preferred_element_type=jnp.float32)
    for q in range(group):
        here = slice(q * capacity, (q + 1) * capacity)
        rows_ref[q] = jnp.where(tops[q], looked[here, width:], looked[here, :width]).astype(bf16)
    summed = jnp.dot(spread[...], jnp.concatenate(doubled, axis=0), preferred_element_type=jnp.float32)

    @pl.when(pl.program_id(0) == 0)
    def _():
        part_ref[0] = summed[:, :width]
        part_ref[1] = summed[:, width:]

    @pl.when(pl.program_id(0) > 0)
    def _():
        part_ref[0] += summed[:, :width]
        part_ref[1] += summed[:, width:]


def per_device(n, table, accum, request_ids, send_counts, entry_slots, entry_weights, pooled_grad):
    r = lax.axis_index("replica")
    rows, width = table.shape
    _, peers, capacity = request_ids.shape
    slots = peers * capacity
    samples, bag = entry_slots.shape
    unit = rows // n
    bf16, f32 = jnp.bfloat16, jnp.float32
    anywhere = pl.BlockSpec(memory_space=pl.ANY)
    vmem = pl.BlockSpec(memory_space=pltpu.VMEM)
    dma = pltpu.SemaphoreType.DMA
    by_owner = (SIDE, SIDE, 2)
    by_core = (2, SIDE, SIDE)
    by_y = (SIDE, SIDE, 2)

    block = 512
    inc, slot_grad = pl.pallas_call(
        functools.partial(incidence, capacity),
        grid=(slots // block,),
        in_specs=[
            pl.BlockSpec(memory_space=pltpu.SMEM),
            pl.BlockSpec((bag, samples), lambda i: (0, 0)),
            pl.BlockSpec((bag, samples), lambda i: (0, 0)),
            pl.BlockSpec((samples, width), lambda i: (0, 0)),
        ],
        out_specs=[pl.BlockSpec((block, samples), lambda i: (i, 0)), pl.BlockSpec((block, width), lambda i: (i, 0))],
        out_shape=[jax.ShapeDtypeStruct((slots, samples), bf16), jax.ShapeDtypeStruct((slots, width), bf16)],
        scratch_shapes=[pltpu.VMEM((bag, capacity, samples), f32)],
        name="incidence",
    )(send_counts.reshape(peers), entry_slots.T, entry_weights.T, pooled_grad)

    piece = lax.dynamic_slice(table, (r * unit, 0), (unit, width)).astype(bf16)
    whole, ids, grads = pl.pallas_call(
        functools.partial(inward, n),
        in_specs=[vmem, vmem, anywhere],
        out_specs=[vmem, vmem, anywhere],
        out_shape=[
            jax.ShapeDtypeStruct((n, unit, width), bf16),
            jax.ShapeDtypeStruct(by_core + (1, capacity), jnp.int32),
            jax.ShapeDtypeStruct(by_core + (capacity, width), bf16),
        ],
        scratch_shapes=[
            pltpu.VMEM(by_owner + (1, capacity), jnp.int32),
            pltpu.VMEM(by_y + (1, capacity), jnp.int32),
            pltpu.VMEM(by_owner + (capacity // 2, width), bf16),
            pltpu.VMEM(by_y + (capacity // 2, width), bf16),
            pltpu.VMEM(by_y + (capacity, width), bf16),
            dma((3,)), dma((8,)), dma((FAR,)), dma((FAR,)), dma((4,)), dma((4,)),
            dma((2 * SIDE,)), dma((2 * SIDE,)), dma((4 * SIDE,)), dma((4 * SIDE,)),
        ],
        compiler_params=pltpu.CompilerParams(collective_id=0, has_side_effects=True, vmem_limit_bytes=16 << 20),
        name="inward",
    )(piece, request_ids.reshape(by_owner + (1, capacity)), slot_grad.reshape(by_owner + (capacity, width)))

    group = 4
    halves = whole.reshape(2, rows // 2, width)
    looked, part = pl.pallas_call(
        lookup_and_sum,
        grid=(peers // group,),
        in_specs=[
            pl.BlockSpec((group, 1, capacity), lambda i: (i, 0, 0)),
            pl.BlockSpec((group, capacity, width), lambda i: (i, 0, 0)),
            pl.BlockSpec((rows // 2, 2 * width), lambda i: (0, 0)),
        ],
        out_specs=[
            pl.BlockSpec((group, capacity, width), lambda i: (i, 0, 0)),
            pl.BlockSpec((2, rows // 2, width), lambda i: (0, 0, 0)),
        ],
        out_shape=[
            jax.ShapeDtypeStruct((peers, capacity, width), bf16),
            jax.ShapeDtypeStruct((2, rows // 2, width), f32),
        ],
        scratch_shapes=[
            pltpu.VMEM((group * capacity, rows // 2), bf16),
            pltpu.VMEM((rows // 2, group * capacity), bf16),
        ],
        compiler_params=pltpu.CompilerParams(vmem_limit_bytes=32 << 20),
        name="lookup_and_sum",
    )(ids.reshape(peers, 1, capacity), grads.reshape(peers, capacity, width),
      jnp.concatenate([halves[0], halves[1]], axis=1))

    arrived, grad = pl.pallas_call(
        functools.partial(outward, n),
        in_specs=[vmem, anywhere],
        out_specs=[anywhere, vmem],
        out_shape=[
            jax.ShapeDtypeStruct(by_owner + (capacity, width), bf16),
            jax.ShapeDtypeStruct(by_owner + (unit, width), f32),
        ],
        scratch_shapes=[
            pltpu.VMEM(by_core + (capacity, width), bf16),
            pltpu.VMEM((SIDE, 2, SIDE, capacity // 2, width), bf16),
            pltpu.VMEM((SIDE, 2, SIDE, capacity // 2, width), bf16),
            pltpu.VMEM((FAR, unit, width), f32),
            pltpu.VMEM((FAR, unit, width), f32),
            pltpu.VMEM((FAR // 2, unit, width), f32),
            pltpu.VMEM((FAR // 2, unit, width), f32),
            pltpu.VMEM((FAR, unit, width), f32),
            pltpu.VMEM((FAR, unit, width), bf16),
            pltpu.VMEM((FAR, unit, width), bf16),
            pltpu.VMEM((unit, width), f32),
            dma((3,)), dma((5,)), dma((FAR,)), dma((FAR,)), dma((4,)), dma((4,)),
            dma((4 * SIDE,)), dma((4 * SIDE,)), dma((4 * SIDE,)), dma((4 * SIDE,)),
        ],
        compiler_params=pltpu.CompilerParams(collective_id=1, has_side_effects=True, vmem_limit_bytes=16 << 20),
        name="outward",
    )(part.reshape(NEAR, FAR, unit, width), looked.reshape(by_core + (capacity, width)))

    pooled = lax.dot_general(
        inc, arrived.reshape(slots, width), (((0,), (0,)), ((), ())), preferred_element_type=f32
    ).astype(bf16)
    grad = grad.reshape(rows, width)
    fresh = accum + grad * grad
    return pooled, table - learn_rate * grad / jnp.sqrt(fresh), fresh


def solution(mesh):
    n = mesh.shape["mp"]
    both = ("replica", "mp")
    return jax.shard_map(
        functools.partial(per_device, n),
        mesh=mesh,
        in_specs=(
            P("mp", None),
            P("mp", None),
            P(both, None, None),
            P(both, None),
            P(both, None),
            P(both, None),
            P(both, None),
        ),
        out_specs=(P(both, None), P("mp", None), P("mp", None)),
        check_vma=False,
    )
```

time: 574 us -> 163 us (0.28)
  waiting for transfers between devices: 355 us -> 0 us
  Pallas kernels: 0 us -> 154 us
  other arithmetic: 108 us -> 1.81 us
  starting transfers between devices: 60.9 us -> 0 us
  local copies, waits for them, and re-layouts: 22.4 us -> 4.04 us
  between operations: 14.1 us -> 0.7 us
  matrix products: 12 us -> 1.38 us
    all_to_all x3 -> x0, waiting for transfers between devices: 261 us -> none  [the longest x1 180 us: per_device(): lax.all_to_all(slot_grad.reshape(peers, capacity, width), 'mp', split_axi...]
    pallas_call x0 -> x4, Pallas kernels: none -> 154 us  [the longest x1 70.5 us: per_device(): pl.pallas_call(functools.partial(inward, n), in_specs=[vmem, vmem, anywhe...]
    psum x1 -> x0, waiting for transfers between devices: 93.5 us -> none  [per_device(): total = lax.psum(row_grad, 'replica')]
    add x16 -> x0, other arithmetic: 79.6 us -> none  [add_entry(): return incidence + jnp.where(slot_iota == slot_col, weight_col, 0.0)]
    all_to_all x3 -> x0, starting transfers between devices: 60.9 us -> none  [the longest x1 29.4 us: per_device(): lax.all_to_all(asked, 'mp', split_axis=0, concat_axis=0, tiled=True)]
    scatter-add x1 -> x0, other arithmetic: 23.7 us -> none  [per_device(): jax.ops.segment_sum(returned.reshape(-1, width), received.reshape(-1), nu...]
    dynamic_slice x32 -> x0, local copies, waits for them, and re-layouts: 11.3 us -> none  [the longest x16 11.2 us: add_entry(): slot_col = lax.dynamic_slice_in_dim(entry_slots, index, 1, 1)]
    gather x1 -> x0, local copies, waits for them, and re-layouts: 11 us -> none  [per_device(): looked = jnp.take(table, received, axis=0).astype(jnp.bfloat16)]
  transfers between devices with their start and end apart: 4 -> 0, of which waited for: 3 -> 0; matrix products, arithmetic and copies ran while one was open for 24% -> 0% of each run, Pallas kernels for 0% -> 0%
where the time goes in v1:
time: 163 us; the launch traced here: 162 us
  Pallas kernels  154 us (94%)
  local copies, waits for them, and re-layouts  4.04 us (2%)
  other arithmetic  1.81 us (1%)
    pallas_call x1, Pallas kernels, per_device(): pl.pallas_call(functools.partial(inward, n), in_specs=[vmem, vmem, anywhe...  70.5 us
    pallas_call x1, Pallas kernels, per_device(): pl.pallas_call(functools.partial(outward, n), in_specs=[vmem, anywhere],...  65.7 us
    pallas_call x1, Pallas kernels, per_device(): pl.pallas_call(functools.partial(incidence, capacity), grid=(slots // blo...  9.04 us
    pallas_call x1, Pallas kernels, per_device(): pl.pallas_call(lookup_and_sum, grid=(peers // group,), in_specs=[pl.Block...  8.74 us

profile of v1, /device:TPU:1, one launch (start us, length us, event | category | flops | bytes accessed | tf_op | source)
XLA Modules:
  0.0 161.9 jit_solution(13602115735037984356)
XLA Ops:
  0.6 0.8 dynamic-slice_convert_fusion.piece_ref
  1.4 9.0 %incidence.1 = (bf16[4096,256]{1,0:T(8,128)(2,1)}, bf16[4096,128]{1,0:T(8,128)(2,1)}) custom-call(s32[32]{0:T(128)} %bitcast.32, s32[16,256]{1,0:T(8,128)} %bitcast.30, bf16[16,256]{1,0:T(8,128)(2,1)} %bitcast.31, bf16[256,128]{1,0:T(8,128)(2,1)} %cot_ref.1), custom_call_target="tpu_custom_call" | custom-call | tf_op jit(solution)/shard_map/incidence/pallas_call | solution.py:409
  10.4 0.0 copy-start
  10.4 1.2 copy-done
  11.7 0.0 copy-start.1
  11.7 0.7 copy-done.1
  12.4 70.5 %inward.1 = (bf16[32,64,128]{2,1,0:T(8,128)(2,1)S(1)}, s32[2,4,4,1,128]{4,3,2,1,0:T(1,128)S(1)}, bf16[2,4,4,128,128]{4,3,2,1,0:T(8,128)(2,1)S(1)}) custom-call(bf16[64,128]{1,0:T(8,128)(2,1)S(1)} %dynamic-slice_convert_fusion.piece_ref, s32[4,4,2,1,128]{4,3,2,1,0:T(1,128)S(1)} %bitcast.26, bf16[4,4,2,128,128]{4,3,2,1,0:T(8,128)(2,1)S(1)} %bitcast.25), custom_call_target="tpu_custom_call" | custom-call | tf_op jit(solution)/shard_map/inward/pallas_call | solution.py:425
  82.9 0.1 pad_maximum_fusion.table_ref
  83.0 0.0 copy-start.2
  83.0 8.7 %lookup_and_sum.1 = (bf16[32,128,128]{2,1,0:T(8,128)(2,1)S(1)}, f32[2,1024,128]{2,1,0:T(8,128)S(1)}) custom-call(s32[32,1,128]{2,1,0:T(1,128)S(1)} %bitcast.27, bf16[32,128,128]{2,1,0:T(8,128)(2,1)S(1)} %bitcast.22, bf16[1024,256]{1,0:T(8,128)(2,1)S(1)} %pad_maximum_fusion.table_ref), custom_call_target="tpu_custom_call" | custom-call | tf_op jit(solution)/shard_map/lookup_and_sum/pallas_call | solution.py:449
  91.8 65.7 %outward.1 = (bf16[4,4,2,128,128]{4,3,2,1,0:T(8,128)(2,1)S(1)}, f32[4,4,2,64,128]{4,3,2,1,0:T(8,128)S(1)}) custom-call(f32[4,8,64,128]{3,2,1,0:T(8,128)S(1)} %bitcast.24, bf16[2,4,4,128,128]{4,3,2,1,0:T(8,128)(2,1)S(1)} %bitcast.23), custom_call_target="tpu_custom_call" | custom-call | tf_op jit(solution)/shard_map/outward/pallas_call | solution.py:474
  157.5 0.0 copy-done.2
  157.5 1.4 convolution_convert_fusion
  158.8 0.0 copy-start.3
  158.8 0.0 copy-start.4
  158.9 0.2 broadcast_multiply_fusion
  159.1 1.0 copy-done.3
  160.1 0.3 copy-done.4
  160.4 1.5 fusion
  (1 shorter events, 0.0 us)
Async XLA Ops:
  10.4 1.2 copy-start
  11.7 0.7 copy-start.1
  83.0 74.5 %copy-start.2 = (bf16[4096,256]{1,0:T(8,128)(2,1)S(1)}, bf16[4096,256]{1,0:T(8,128)(2,1)}, u32[]{:S(2)}) copy-start(bf16[4096,256]{1,0:T(8,128)(2,1)} %get-tuple-element.12) | copy-start | bytes 6291460
  158.8 1.2 copy-start.3
  158.8 1.5 copy-start.4

commit v2 on v0

v2 whole, which is shorter than its diff:
```python
import functools

import jax
import jax.numpy as jnp
from jax import lax
from jax.experimental import pallas as pl
from jax.experimental.pallas import tpu as pltpu
from jax.sharding import PartitionSpec as P

learn_rate = 0.5
FAR = 8
NEAR = 4
SIDE = 4
MESH = pl.DeviceIdType.MESH


def remote(src, dst, send_sem, recv_sem, r, z):
    return pltpu.make_async_remote_copy(
        src_ref=src, dst_ref=dst, send_sem=send_sem, recv_sem=recv_sem,
        device_id={"replica": r, "mp": z}, device_id_type=MESH,
    )


def place(index):
    return lax.rem(index, NEAR) * FAR + index // NEAR


class Seat:
    def __init__(self, n):
        self.n = n
        self.r, self.z = lax.axis_index("replica"), lax.axis_index("mp")
        self.x, self.y, self.c = self.r // (2 * SIDE), lax.rem(self.r // 2, SIDE), lax.rem(self.r, 2)
        self.a, self.b = self.z // NEAR, lax.rem(self.z, NEAR)
        self.twin = self.r + 1 - 2 * self.c

    def x_at(self, o):
        return lax.rem(self.x + o, SIDE)

    def y_at(self, o):
        return lax.rem(self.y + o, SIDE)

    def along_x(self, o):
        return (self.x_at(o) * SIDE + self.y) * 2 + self.c

    def along_y(self, o):
        return (self.x * SIDE + self.y_at(o)) * 2 + self.c

    def up(self, o):
        return lax.rem(self.z + o + self.n, self.n)

    def greet(self):
        barrier = pltpu.get_barrier_semaphore()

        def hello(r, z):
            pl.semaphore_signal(barrier, inc=1, device_id={"replica": r, "mp": z}, device_id_type=MESH)

        @pl.loop(1, SIDE)
        def _(o):
            hello(self.along_x(o), self.z)
            hello(self.along_y(o), self.z)

        @pl.loop(1, FAR)
        def _(o):
            hello(self.r, self.up(NEAR * o))

        hello(self.twin, self.z)
        for o in (-2, -1, 1, 2):
            hello(self.r, self.up(o))

        @pl.when(self.r != self.z)
        def _():
            hello(self.z, self.r)

        pl.semaphore_wait(barrier, 2 * (SIDE - 1) + FAR - 1 + 5 + jnp.where(self.r != self.z, 1, 0))

    def turn(self, src, dst, dst_local, sems):
        def away():
            return remote(src, dst, sems.at[0], sems.at[1], self.z, self.r)

        def here():
            return pltpu.make_async_copy(src, dst_local, sems.at[2])

        def start():
            @pl.when(self.r != self.z)
            def _():
                away().start()

            @pl.when(self.r == self.z)
            def _():
                here().start()

        def wait():
            @pl.when(self.r != self.z)
            def _():
                away().wait()

            @pl.when(self.r == self.z)
            def _():
                here().wait()

        return start, wait


def start_each(last, *copies):
    @pl.loop(1, last)
    def _(o):
        for copy in copies:
            copy(o).start()


def wait_each(last, *copies):
    @pl.loop(1, last)
    def _(o):
        for copy in copies:
            copy(o).wait()


SUB = 64
GROUP = 4


def step(n, counts_ref, piece_ref, ids_ref, slots_ref, weights_ref, cot_ref, inc_out, rows_out, grad_out,
         hot, inc, slot_grad, table, table_wide, ids_x, ids_y, ids_in, grad_x, grad_y, grad_b, grad_in,
         pick, spread, tops, doubled, part, looked, rows_b, rows_y, rows_x, near_a, near_b, near_c, near_d,
         total, far_out, far_in, piece,
         turn_sem, own_sem, far_sem, near_sem, id_sem, grad_sem, sum_sem, sum_far, row_sem, fin_sem):
    seat = Seat(n)
    r, z, x, y, c, b = seat.r, seat.z, seat.x, seat.y, seat.c, seat.b
    bf16, f32 = jnp.bfloat16, jnp.float32
    bag, capacity, samples = hot.shape
    width = cot_ref.shape[1]
    owners = inc.shape[0] // capacity
    middle, wide = FAR // 2, pick.shape[1]
    unit = piece.shape[0]
    low, high = pl.ds(0, capacity // 2), pl.ds(capacity // 2, capacity // 2)
    seat.greet()

    mine = table.at[place(z)]
    turn_start, turn_wait = seat.turn(piece_ref, table.at[place(r)], mine, turn_sem.at[0])
    turn_start()

    def far(o):
        return remote(mine, mine, far_sem.at[0, o], far_sem.at[1, o], r, seat.up(NEAR * o))

    def near(k, first, count, o):
        block = table.at[pl.ds(b * FAR + first, count)]
        return remote(block, block, near_sem.at[0, k], near_sem.at[1, k], r, seat.up(o))

    nears = [near(0, 0, FAR, 1), near(1, 0, FAR, -1), near(2, 0, middle, 2), near(3, middle, middle, -2)]

    def ship_ids(src, dst, k, to):
        return remote(src, dst, id_sem.at[0, k], id_sem.at[1, k], to, z)

    def x_ids(o):
        return ship_ids(ids_ref.at[seat.x_at(o)], ids_x.at[x], o, seat.along_x(o))

    def y_ids(o):
        return ship_ids(ids_x.at[:, seat.y_at(o)], ids_y.at[y], SIDE + o, seat.along_y(o))

    twin_ids = ship_ids(ids_y.at[:, :, 1 - c], ids_in.at[c], 0, seat.twin)

    def ship(src, dst, k, to):
        return remote(src, dst, grad_sem.at[0, k], grad_sem.at[1, k], to, z)

    def x_low(o):
        return ship(slot_grad.at[seat.x_at(o), :, :, low], grad_x.at[x], o, seat.along_x(o))

    def y_high(o):
        return ship(slot_grad.at[:, seat.y_at(o), :, high], grad_y.at[y], SIDE + o, seat.along_y(o))

    def y_low(o):
        return ship(grad_x.at[:, seat.y_at(o)], grad_b.at[y, :, :, low], 2 * SIDE + o, seat.along_y(o))

    def x_high(o):
        return ship(grad_y.at[:, seat.x_at(o)], grad_b.at[:, x, :, high], 3 * SIDE + o, seat.along_x(o))

    twin_grad = ship(grad_b.at[:, :, 1 - c], grad_in.at[c], 0, seat.twin)

    def ship_rows(src, dst, k, to):
        return remote(src, dst, row_sem.at[0, k], row_sem.at[1, k], to, z)

    def y_low_rows(o):
        return ship_rows(rows_b.at[:, seat.y_at(o), :, low], rows_y.at[y], o, seat.along_y(o))

    def x_high_rows(o):
        return ship_rows(rows_b.at[:, :, seat.x_at(o), high], rows_x.at[x], SIDE + o, seat.along_x(o))

    def x_low_rows(o):
        return ship_rows(rows_y.at[:, :, seat.x_at(o)], rows_out.at[x, :, :, low], 2 * SIDE + o, seat.along_x(o))

    def y_high_rows(o):
        return ship_rows(rows_x.at[:, :, seat.y_at(o)], rows_out.at[:, y, :, high], 3 * SIDE + o, seat.along_y(o))

    twin_rows = ship_rows(looked.at[1 - c], rows_b.at[c], 0, seat.twin)

    own = [pltpu.make_async_copy(src, dst, own_sem.at[k]) for k, (src, dst) in enumerate((
        (ids_ref.at[x], ids_x.at[x]),
        (ids_x.at[:, y], ids_y.at[y]),
        (ids_y.at[:, :, c], ids_in.at[c]),
        (slot_grad.at[x, :, :, low], grad_x.at[x]),
        (slot_grad.at[:, y, :, high], grad_y.at[y]),
        (grad_x.at[:, y], grad_b.at[y, :, :, low]),
        (grad_y.at[:, x], grad_b.at[:, x, :, high]),
        (grad_b.at[:, :, c], grad_in.at[c]),
        (looked.at[c], rows_b.at[c]),
        (rows_b.at[:, y, :, low], rows_y.at[y]),
        (rows_b.at[:, :, x, high], rows_x.at[x]),
        (rows_y.at[:, :, x], rows_out.at[x, :, :, low]),
        (rows_x.at[:, :, y], rows_out.at[:, y, :, high]),
        (inc, inc_out),
    ))]

    def start_own(*which):
        for k in which:
            own[k].start()

    def wait_own(*which):
        for k in which:
            own[k].wait()

    def incidence(first, last):
        @pl.loop(first, last)
        def _(owner):
            weights = jnp.where(slots_ref[...] // capacity == owner, weights_ref[...].astype(f32), 0.0)
            for at in range(0, capacity, SUB):
                acc = hot[0, at:at + SUB] * weights[0:1, :]
                for entry in range(1, bag):
                    acc += hot[entry, at:at + SUB] * weights[entry:entry + 1, :]
                slot = at + lax.broadcasted_iota(jnp.int32, (SUB, samples), 0)
                acc = jnp.where(slot < counts_ref[owner], acc, 0.0)
                inc[pl.ds(pl.multiple_of(owner * capacity + at, SUB), SUB), :] = acc.astype(bf16)

    def slot_sums(first, last):
        @pl.loop(first, last)
        def _(k):
            size = GROUP * capacity
            block = inc[pl.ds(pl.multiple_of(k * size, size), size), :]
            sums = jnp.dot(block, cot_ref[...], preferred_element_type=f32).astype(bf16)
            half_side = SIDE // 2
            slot_grad[k // half_side, pl.ds(lax.rem(k, half_side) * half_side, half_side)] = sums.reshape(
                half_side, 2, capacity, width)

    def masks(first, last):
        one, zero = jnp.ones((capacity, 128), bf16), jnp.zeros((capacity, 128), bf16)
        lane = lax.broadcasted_iota(jnp.int32, (capacity, 128), 1).astype(f32).astype(bf16)
        row = lax.broadcasted_iota(jnp.int32, (128, capacity), 0).astype(f32).astype(bf16)

        def split(ids):
            lows = jnp.bitwise_and(ids, 127).astype(f32).astype(bf16)
            mids = jnp.bitwise_and(lax.shift_right_logical(ids, 7), wide // 128 - 1).astype(f32).astype(bf16)
            return lows, mids

        @pl.loop(first, last)
        def _(q):
            spot = ids_in[q // (SIDE * SIDE), lax.rem(q // SIDE, SIDE), lax.rem(q, SIDE)]
            spot = (lax.rem(spot // unit, NEAR) * FAR + spot // (unit * NEAR)) * unit + lax.rem(spot, unit)
            ids = jnp.broadcast_to(spot, (capacity, capacity))
            column = ids.astype(f32).T.astype(jnp.int32)
            here = pl.ds(pl.multiple_of(q * capacity, capacity), capacity)
            lows, mids = split(column)
            lit = jnp.where(lane == lows, one, zero)
            for tile in range(wide // 128):
                pick[here, tile * 128:(tile + 1) * 128] = jnp.where(mids == jnp.full_like(mids, tile), lit, zero)
            tops[here, :] = jnp.where(column >= wide, 1.0, 0.0)
            lows, mids = split(ids)
            lit = jnp.where(row == lows, one, zero)
            for tile in range(wide // 128):
                spread[tile * 128:(tile + 1) * 128, here] = jnp.where(mids == jnp.full_like(mids, tile), lit, zero)

    def sum_rows():
        @pl.loop(0, owners)
        def _(q):
            here = pl.ds(pl.multiple_of(q * capacity, capacity), capacity)
            cot = grad_in[q // (SIDE * SIDE), lax.rem(q // SIDE, SIDE), lax.rem(q, SIDE)].astype(f32)
            top = tops[here, :] > 0.5
            doubled[here, 0:width] = jnp.where(top, 0.0, cot).astype(bf16)
            doubled[here, width:2 * width] = jnp.where(top, cot, 0.0).astype(bf16)

        for k in range(NEAR // 2):
            size = FAR * unit
            sums = jnp.dot(spread[k * size:(k + 1) * size, :], doubled[...], preferred_element_type=f32)
            part[k] = sums[:, :width].reshape(FAR, unit, width)
            part[k + NEAR // 2] = sums[:, width:].reshape(FAR, unit, width)

    def look_up():
        table_wide[:, 0:width] = table[0:owners // 2].reshape(wide, width)
        table_wide[:, width:2 * width] = table[owners // 2:owners].reshape(wide, width)

        @pl.loop(0, owners // GROUP)
        def _(k):
            size = GROUP * capacity
            here = pl.ds(pl.multiple_of(k * size, size), size)
            both = jnp.dot(pick[here, :], table_wide[...], preferred_element_type=f32)
            rows = jnp.where(tops[here, :] > 0.5, both[:, width:], both[:, :width]).astype(bf16)
            looked[k // SIDE, lax.rem(k, SIDE)] = rows.reshape(SIDE, capacity, width)

    start_each(SIDE, x_ids)
    start_own(0)
    low_slot = lax.broadcasted_iota(jnp.int32, (capacity, samples), 0)
    for entry in range(bag):
        hot[entry] = jnp.where(low_slot == lax.rem(slots_ref[entry:entry + 1, :], capacity), 1.0, 0.0)
    incidence(0, owners // 2)
    turn_wait()
    start_each(FAR, far)
    wait_own(0)
    wait_each(SIDE, x_ids)
    start_each(SIDE, y_ids)
    start_own(1)
    incidence(owners // 2, owners)
    slot_sums(0, owners // GROUP)
    start_each(SIDE, x_low, y_high)
    start_own(3, 4, 13)
    wait_own(1)
    wait_each(SIDE, y_ids)
    twin_ids.start()
    start_own(2)
    wait_own(2)
    twin_ids.wait()
    masks(0, owners // 2)
    wait_own(3, 4)
    wait_each(SIDE, x_low, y_high)
    start_each(SIDE, y_low, x_high)
    start_own(5, 6)
    wait_each(FAR, far)
    for copy in nears:
        copy.start()
    masks(owners // 2, owners)
    wait_own(5, 6)
    wait_each(SIDE, y_low, x_high)
    twin_grad.start()
    start_own(7)
    wait_own(7)
    twin_grad.wait()
    sum_rows()

    def sum_near(k, first, count, o, dst):
        block = part.at[lax.rem(b + o + NEAR, NEAR), pl.ds(first, count)]
        return remote(block, dst, sum_sem.at[0, k], sum_sem.at[1, k], r, seat.up(o))

    sum_nears = [sum_near(0, 0, FAR, 1, near_a), sum_near(1, 0, FAR, -1, near_b),
                 sum_near(2, 0, middle, 2, near_c), sum_near(3, middle, middle, -2, near_d)]

    def sum_far_copy(o):
        return remote(far_out.at[lax.rem(seat.a + o, FAR)], far_in.at[o], sum_far.at[0, o], sum_far.at[1, o],
                      r, seat.up(NEAR * o))

    for copy in sum_nears:
        copy.start()
    for copy in nears:
        copy.wait()
    look_up()
    twin_rows.start()
    start_own(8)
    wait_own(8)
    twin_rows.wait()
    start_each(SIDE, y_low_rows, x_high_rows)
    start_own(9, 10)
    for copy in sum_nears:
        copy.wait()
    for first, far_half in ((0, near_c), (middle, near_d)):
        here = pl.ds(first, middle)
        total[here] = (part[b, here] + near_a[here]) + (near_b[here] + far_half[...])
    far_out[...] = total[...].astype(bf16)
    start_each(FAR, sum_far_copy)
    wait_own(9, 10)
    wait_each(SIDE, y_low_rows, x_high_rows)
    start_each(SIDE, x_low_rows, y_high_rows)
    start_own(11, 12)
    wait_each(FAR, sum_far_copy)
    far_sum = total[seat.a]
    for o in range(1, FAR):
        far_sum = far_sum + far_in[o].astype(f32)
    piece[...] = far_sum

    afar = grad_out.at[z // (2 * SIDE), lax.rem(z // 2, SIDE), lax.rem(z, 2)]
    back_start, back_wait = seat.turn(piece, afar, grad_out.at[x, y, c], turn_sem.at[1])
    back_start()
    wait_own(11, 12, 13)
    wait_each(SIDE, x_low_rows, y_high_rows)
    back_wait()

    upper, lower = pl.ds(0, unit // 2), pl.ds(unit // 2, unit // 2)

    def share(ref, k, to):
        return remote(ref, ref, fin_sem.at[0, k], fin_sem.at[1, k], to, z)

    def x_upper(o):
        return share(grad_out.at[x, y, c, upper], o, seat.along_x(o))

    def y_lower(o):
        return share(grad_out.at[x, y, c, lower], SIDE + o, seat.along_y(o))

    def y_upper(o):
        return share(grad_out.at[:, y, c, upper], 2 * SIDE + o, seat.along_y(o))

    def x_lower(o):
        return share(grad_out.at[x, :, c, lower], 3 * SIDE + o, seat.along_x(o))

    start_each(SIDE, x_upper, y_lower)
    wait_each(SIDE, x_upper, y_lower)
    start_each(SIDE, y_upper, x_lower)
    wait_each(SIDE, y_upper, x_lower)
    last = share(grad_out.at[:, :, c], 0, seat.twin)
    last.start()
    last.wait()


def per_device(n, table, accum, request_ids, send_counts, entry_slots, entry_weights, pooled_grad):
    r = lax.axis_index("replica")
    rows, width = table.shape
    _, peers, capacity = request_ids.shape
    slots = peers * capacity
    samples, bag = entry_slots.shape
    unit = rows // n
    bf16, f32, i32 = jnp.bfloat16, jnp.float32, jnp.int32
    anywhere = pl.BlockSpec(memory_space=pl.ANY)
    vmem = pl.BlockSpec(memory_space=pltpu.VMEM)
    dma = pltpu.SemaphoreType.DMA
    by_owner = (SIDE, SIDE, 2)
    by_core = (2, SIDE, SIDE)
    by_line = (SIDE, 2, SIDE)
    cut = capacity // 2

    piece = lax.dynamic_slice(table, (r * unit, 0), (unit, width)).astype(bf16)
    inc, arrived, grad = pl.pallas_call(
        functools.partial(step, n),
        in_specs=[pl.BlockSpec(memory_space=pltpu.SMEM), vmem, vmem, vmem, vmem, vmem],
        out_specs=[anywhere, anywhere, vmem],
        out_shape=[
            jax.ShapeDtypeStruct((slots, samples), bf16),
            jax.ShapeDtypeStruct(by_owner + (capacity, width), bf16),
            jax.ShapeDtypeStruct(by_owner + (unit, width), f32),
        ],
        scratch_shapes=[
            pltpu.VMEM((bag, capacity, samples), f32),
            pltpu.VMEM((slots, samples), bf16),
            pltpu.VMEM(by_owner + (capacity, width), bf16),
            pltpu.VMEM((n, unit, width), bf16),
            pltpu.VMEM((rows // 2, 2 * width), bf16),
            pltpu.VMEM(by_owner + (1, capacity), i32),
            pltpu.VMEM(by_owner + (1, capacity), i32),
            pltpu.VMEM(by_core + (1, capacity), i32),
            pltpu.VMEM(by_owner + (cut, width), bf16),
            pltpu.VMEM(by_owner + (cut, width), bf16),
            pltpu.VMEM(by_owner + (capacity, width), bf16),
            pltpu.VMEM(by_core + (capacity, width), bf16),
            pltpu.VMEM((slots, rows // 2), bf16),
            pltpu.VMEM((rows // 2, slots), bf16),
            pltpu.VMEM((slots, width), f32),
            pltpu.VMEM((slots, 2 * width), bf16),
            pltpu.VMEM((NEAR, FAR, unit, width), f32),
            pltpu.VMEM(by_core + (capacity, width), bf16),
            pltpu.VMEM(by_core + (capacity, width), bf16),
            pltpu.VMEM(by_line + (cut, width), bf16),
            pltpu.VMEM(by_line + (cut, width), bf16),
            pltpu.VMEM((FAR, unit, width), f32),
            pltpu.VMEM((FAR, unit, width), f32),
            pltpu.VMEM((FAR // 2, unit, width), f32),
            pltpu.VMEM((FAR // 2, unit, width), f32),
            pltpu.VMEM((FAR, unit, width), f32),
            pltpu.VMEM((FAR, unit, width), bf16),
            pltpu.VMEM((FAR, unit, width), bf16),
            pltpu.VMEM((unit, width), f32),
            dma((2, 3)), dma((14,)), dma((2, FAR)), dma((2, 4)), dma((2, 2 * SIDE)), dma((2, 4 * SIDE)),
            dma((2, 4)), dma((2, FAR)), dma((2, 4 * SIDE)), dma((2, 4 * SIDE)),
        ],
        compiler_params=pltpu.CompilerParams(collective_id=0, has_side_effects=True, vmem_limit_bytes=48 << 20),
        name="step",
    )(send_counts.reshape(peers), piece, request_ids.reshape(by_owner + (1, capacity)),
      entry_slots.T, entry_weights.T, pooled_grad)

    pooled = lax.dot_general(
        inc, arrived.reshape(slots, width), (((0,), (0,)), ((), ())), preferred_element_type=f32
    ).astype(bf16)
    grad = grad.reshape(rows, width)
    fresh = accum + grad * grad
    return pooled, table - learn_rate * grad / jnp.sqrt(fresh), fresh


def solution(mesh):
    n = mesh.shape["mp"]
    both = ("replica", "mp")
    return jax.shard_map(
        functools.partial(per_device, n),
        mesh=mesh,
        in_specs=(
            P("mp", None),
            P("mp", None),
            P(both, None, None),
            P(both, None),
            P(both, None),
            P(both, None),
            P(both, None),
        ),
        out_specs=(P(both, None), P("mp", None), P("mp", None)),
        check_vma=False,
    )
```

time: 574 us -> 144 us (0.25)
  waiting for transfers between devices: 355 us -> 0 us
  Pallas kernels: 0 us -> 134 us
  other arithmetic: 108 us -> 1.75 us
  starting transfers between devices: 60.9 us -> 0 us
  local copies, waits for them, and re-layouts: 22.4 us -> 5.68 us
  between operations: 14.1 us -> 0.66 us
  matrix products: 12 us -> 1.38 us
    all_to_all x3 -> x0, waiting for transfers between devices: 261 us -> none  [the longest x1 180 us: per_device(): lax.all_to_all(slot_grad.reshape(peers, capacity, width), 'mp', split_axi...]
    pallas_call x0 -> x1, Pallas kernels: none -> 134 us  [per_device(): pl.pallas_call(functools.partial(step, n), in_specs=[pl.BlockSpec(memory_...]
    psum x1 -> x0, waiting for transfers between devices: 93.5 us -> none  [per_device(): total = lax.psum(row_grad, 'replica')]
    add x16 -> x0, other arithmetic: 79.6 us -> none  [add_entry(): return incidence + jnp.where(slot_iota == slot_col, weight_col, 0.0)]
    all_to_all x3 -> x0, starting transfers between devices: 60.9 us -> none  [the longest x1 29.4 us: per_device(): lax.all_to_all(asked, 'mp', split_axis=0, concat_axis=0, tiled=True)]
    scatter-add x1 -> x0, other arithmetic: 23.7 us -> none  [per_device(): jax.ops.segment_sum(returned.reshape(-1, width), received.reshape(-1), nu...]
    dynamic_slice x32 -> x0, local copies, waits for them, and re-layouts: 11.3 us -> none  [the longest x16 11.2 us: add_entry(): slot_col = lax.dynamic_slice_in_dim(entry_slots, index, 1, 1)]
    gather x1 -> x0, local copies, waits for them, and re-layouts: 11 us -> none  [per_device(): looked = jnp.take(table, received, axis=0).astype(jnp.bfloat16)]
  transfers between devices with their start and end apart: 4 -> 0, of which waited for: 3 -> 0; matrix products, arithmetic and copies ran while one was open for 24% -> 0% of each run, Pallas kernels for 0% -> 0%
where the time goes in v2:
time: 144 us; the launch traced here: 143 us
  Pallas kernels  134 us (93%)
  local copies, waits for them, and re-layouts  5.68 us (4%)
  other arithmetic  1.75 us (1%)
    pallas_call x1, Pallas kernels, per_device(): pl.pallas_call(functools.partial(step, n), in_specs=[pl.BlockSpec(memory_...  134 us
    unnamed x14, local copies, waits for them, and re-layouts  4.91 us

profile of v2, /device:TPU:1, one launch (start us, length us, event | category | flops | bytes accessed | tf_op | source)
XLA Modules:
  0.0 143.2 jit_solution(7948637522382733402)
XLA Ops:
  0.6 0.8 dynamic-slice_convert_fusion.piece_ref
  1.4 0.0 copy-start
  1.4 0.8 copy-done
  2.2 0.0 copy-start.1
  2.2 0.7 copy-done.1
  3.0 0.0 copy-start.2
  3.0 0.7 copy-done.2
  3.7 0.0 copy-start.3
  3.7 0.7 copy-done.3
  4.4 0.0 copy-start.4
  4.4 0.7 copy-done.4
  5.0 133.7 %step.1 = (bf16[4096,256]{1,0:T(8,128)(2,1)S(1)}, bf16[4,4,2,128,128]{4,3,2,1,0:T(8,128)(2,1)S(1)}, f32[4,4,2,64,128]{4,3,2,1,0:T(8,128)S(1)}) custom-call(s32[32]{0:T(128)S(1)} %bitcast.18, bf16[64,128]{1,0:T(8,128)(2,1)S(1)} %dynamic-slice_convert_fusion.piece_ref, s32[4,4,2,1,128]{4,3,2,1,0:T(1,128)S(1)} %bitcast.15, s32[16,256]{1,0:T(8,128)S(1)} %bitcast.16, ...), custom_call_target="tpu_custom_call" | custom-call | tf_op jit(solution)/shard_map/step/pallas_call | solution.py:425
  138.8 1.4 convolution_convert_fusion
  140.2 0.0 copy-start.5
  140.2 0.0 copy-start.6
  140.2 0.2 broadcast_multiply_fusion
  140.4 1.0 copy-done.5
  141.4 0.3 copy-done.6
  141.7 1.5 %fusion = (f32[2048,128]{1,0:T(8,128)}, f32[2048,128]{1,0:T(8,128)}) fusion(f32[2048,128]{1,0:T(8,128)S(1)} %copy-done.5, f32[4,4,2,64,128]{4,3,2,1,0:T(8,128)S(1)} %get-tuple-element.11, f32[2048,128]{1,0:T(8,128)S(1)} %copy-done.6, f32[4,4,2,64,128]{4,3,2,1,0:T(8,128)S(1)} %get-tuple-element.12), kind=kLoop, calls=%fused_computation.3 | loop fusion | flops 786432 | bytes 6291456 | tf_op jit(solution)/shard_map/sub | solution.py:477
Async XLA Ops:
  1.4 0.8 copy-start
  2.2 0.7 copy-start.1
  3.0 0.7 copy-start.2
  3.7 0.7 copy-start.3
  4.4 0.7 copy-start.4
  140.2 1.2 copy-start.5
  140.2 1.5 %copy-start.6 = (f32[2048,128]{1,0:T(8,128)S(1)}, f32[2048,128]{1,0:T(8,128)}, u32[]{:S(2)}) copy-start(f32[2048,128]{1,0:T(8,128)} %param.8) | copy-start | bytes 3145732

commit v3 on v2

--- a/solution.py
+++ b/solution.py
@@ -116,24 +116,37 @@
 
 
 SUB = 64
+PACK = 16
 GROUP = 4
 
 
-def step(n, counts_ref, piece_ref, ids_ref, slots_ref, weights_ref, cot_ref, inc_out, rows_out, grad_out,
-         hot, inc, slot_grad, table, table_wide, ids_x, ids_y, ids_in, grad_x, grad_y, grad_b, grad_in,
-         pick, spread, tops, doubled, part, looked, rows_b, rows_y, rows_x, near_a, near_b, near_c, near_d,
+def step(n, counts_ref, table_ref, ids_ref, slots_hbm, weights_hbm, cot_hbm, pooled_out, grad_out,
+         fetched, piece_ref, slots_ref, weights_ref, cot_ref, hot, inc, slot_grad, table, table_wide, ids_x, ids_y, ids_in, grad_x, grad_y, grad_b, grad_in,
+         pick, spread, tops, doubled, part, looked, rows_out, rows_b, rows_y, rows_x, near_a, near_b, near_c, near_d,
          total, far_out, far_in, piece,
-         turn_sem, own_sem, far_sem, near_sem, id_sem, grad_sem, sum_sem, sum_far, row_sem, fin_sem):
+         turn_sem, own_sem, far_sem, near_sem, id_sem, grad_sem, sum_sem, sum_far, row_sem, fin_sem, fetch_sem):
     seat = Seat(n)
     r, z, x, y, c, b = seat.r, seat.z, seat.x, seat.y, seat.c, seat.b
     bf16, f32 = jnp.bfloat16, jnp.float32
-    bag, capacity, samples = hot.shape
+    bag, samples = slots_ref.shape
+    capacity = hot.shape[1] * PACK
     width = cot_ref.shape[1]
     owners = inc.shape[0] // capacity
     middle, wide = FAR // 2, pick.shape[1]
     unit = piece.shape[0]
     low, high = pl.ds(0, capacity // 2), pl.ds(capacity // 2, capacity // 2)
+    fetches = [pltpu.make_async_copy(src, dst, fetch_sem.at[k]) for k, (src, dst) in enumerate((
+        (table_ref.at[pl.ds(pl.multiple_of(r * unit, unit), unit)], fetched),
+        (slots_hbm, slots_ref),
+        (weights_hbm, weights_ref),
+        (cot_hbm, cot_ref),
+    ))]
+    for fetch in fetches:
+        fetch.start()
     seat.greet()
+    for fetch in fetches:
+        fetch.wait()
+    piece_ref[...] = fetched[...].astype(bf16)
 
     mine = table.at[place(z)]
     turn_start, turn_wait = seat.turn(piece_ref, table.at[place(r)], mine, turn_sem.at[0])
@@ -207,7 +220,6 @@
         (rows_b.at[:, :, x, high], rows_x.at[x]),
         (rows_y.at[:, :, x], rows_out.at[x, :, :, low]),
         (rows_x.at[:, :, y], rows_out.at[:, y, :, high]),
-        (inc, inc_out),
     ))]
 
     def start_own(*which):
@@ -219,16 +231,25 @@
             own[k].wait()
 
     def incidence(first, last):
+        tiles = SUB // PACK
+
         @pl.loop(first, last)
         def _(owner):
             weights = jnp.where(slots_ref[...] // capacity == owner, weights_ref[...].astype(f32), 0.0)
-            for at in range(0, capacity, SUB):
-                acc = hot[0, at:at + SUB] * weights[0:1, :]
-                for entry in range(1, bag):
-                    acc += hot[entry, at:at + SUB] * weights[entry:entry + 1, :]
-                slot = at + lax.broadcasted_iota(jnp.int32, (SUB, samples), 0)
+            scales = [jnp.broadcast_to(weights[entry:entry + 1, :], (PACK, samples)).astype(bf16)[None]
+                      for entry in range(bag)]
+
+            def entries(at, lower, upper):
+                if upper - lower == 1:
+                    return hot[lower, at:at + tiles] * scales[lower]
+                middle_entry = (lower + upper) // 2
+                return entries(at, lower, middle_entry) + entries(at, middle_entry, upper)
+
+            for at in range(0, capacity // PACK, tiles):
+                slot = at * PACK + lax.broadcasted_iota(jnp.int32, (SUB, samples), 0)
+                acc = entries(at, 0, bag).reshape(SUB, samples).astype(f32)
                 acc = jnp.where(slot < counts_ref[owner], acc, 0.0)
-                inc[pl.ds(pl.multiple_of(owner * capacity + at, SUB), SUB), :] = acc.astype(bf16)
+                inc[pl.ds(pl.multiple_of(owner * capacity + at * PACK, SUB), SUB), :] = acc.astype(bf16)
 
     def slot_sums(first, last):
         @pl.loop(first, last)
@@ -294,11 +315,22 @@
             rows = jnp.where(tops[here, :] > 0.5, both[:, width:], both[:, :width]).astype(bf16)
             looked[k // SIDE, lax.rem(k, SIDE)] = rows.reshape(SIDE, capacity, width)
 
+    def pool():
+        def add(k, acc):
+            size = 2 * GROUP * capacity
+            block = inc[pl.ds(pl.multiple_of(k * size, size), size), :]
+            rows = rows_out[k].reshape(size, width)
+            return acc + lax.dot_general(block, rows, (((0,), (0,)), ((), ())), preferred_element_type=f32)
+
+        pooled = lax.fori_loop(0, SIDE, add, jnp.zeros((samples, width), f32))
+        pooled_out[...] = pooled.astype(bf16)
+
     start_each(SIDE, x_ids)
     start_own(0)
     low_slot = lax.broadcasted_iota(jnp.int32, (capacity, samples), 0)
     for entry in range(bag):
-        hot[entry] = jnp.where(low_slot == lax.rem(slots_ref[entry:entry + 1, :], capacity), 1.0, 0.0)
+        lit = jnp.where(low_slot == lax.rem(slots_ref[entry:entry + 1, :], capacity), 1.0, 0.0)
+        hot[entry] = lit.astype(bf16).reshape(capacity // PACK, PACK, samples)
     incidence(0, owners // 2)
     turn_wait()
     start_each(FAR, far)
@@ -309,7 +341,7 @@
     incidence(owners // 2, owners)
     slot_sums(0, owners // GROUP)
     start_each(SIDE, x_low, y_high)
-    start_own(3, 4, 13)
+    start_own(3, 4)
     wait_own(1)
     wait_each(SIDE, y_ids)
     twin_ids.start()
@@ -375,8 +407,9 @@
     afar = grad_out.at[z // (2 * SIDE), lax.rem(z // 2, SIDE), lax.rem(z, 2)]
     back_start, back_wait = seat.turn(piece, afar, grad_out.at[x, y, c], turn_sem.at[1])
     back_start()
-    wait_own(11, 12, 13)
+    wait_own(11, 12)
     wait_each(SIDE, x_low_rows, y_high_rows)
+    pool()
     back_wait()
 
     upper, lower = pl.ds(0, unit // 2), pl.ds(unit // 2, unit // 2)
@@ -406,33 +439,35 @@
 
 
 def per_device(n, table, accum, request_ids, send_counts, entry_slots, entry_weights, pooled_grad):
-    r = lax.axis_index("replica")
     rows, width = table.shape
     _, peers, capacity = request_ids.shape
     slots = peers * capacity
     samples, bag = entry_slots.shape
     unit = rows // n
     bf16, f32, i32 = jnp.bfloat16, jnp.float32, jnp.int32
-    anywhere = pl.BlockSpec(memory_space=pl.ANY)
     vmem = pl.BlockSpec(memory_space=pltpu.VMEM)
+    hbm = pl.BlockSpec(memory_space=pltpu.HBM)
     dma = pltpu.SemaphoreType.DMA
     by_owner = (SIDE, SIDE, 2)
     by_core = (2, SIDE, SIDE)
     by_line = (SIDE, 2, SIDE)
     cut = capacity // 2
 
-    piece = lax.dynamic_slice(table, (r * unit, 0), (unit, width)).astype(bf16)
-    inc, arrived, grad = pl.pallas_call(
+    pooled, grad = pl.pallas_call(
         functools.partial(step, n),
-        in_specs=[pl.BlockSpec(memory_space=pltpu.SMEM), vmem, vmem, vmem, vmem, vmem],
-        out_specs=[anywhere, anywhere, vmem],
+        in_specs=[pl.BlockSpec(memory_space=pltpu.SMEM), hbm, hbm, hbm, hbm, hbm],
+        out_specs=[vmem, vmem],
         out_shape=[
-            jax.ShapeDtypeStruct((slots, samples), bf16),
-            jax.ShapeDtypeStruct(by_owner + (capacity, width), bf16),
+            jax.ShapeDtypeStruct((samples, width), bf16),
             jax.ShapeDtypeStruct(by_owner + (unit, width), f32),
         ],
         scratch_shapes=[
-            pltpu.VMEM((bag, capacity, samples), f32),
+            pltpu.VMEM((unit, width), f32),
+            pltpu.VMEM((unit, width), bf16),
+            pltpu.VMEM((bag, samples), i32),
+            pltpu.VMEM((bag, samples), bf16),
+            pltpu.VMEM((samples, width), bf16),
+            pltpu.VMEM((bag, capacity // PACK, PACK, samples), bf16),
             pltpu.VMEM((slots, samples), bf16),
             pltpu.VMEM(by_owner + (capacity, width), bf16),
             pltpu.VMEM((n, unit, width), bf16),
@@ -450,6 +485,7 @@
             pltpu.VMEM((slots, 2 * width), bf16),
             pltpu.VMEM((NEAR, FAR, unit, width), f32),
             pltpu.VMEM(by_core + (capacity, width), bf16),
+            pltpu.VMEM(by_owner + (capacity, width), bf16),
             pltpu.VMEM(by_core + (capacity, width), bf16),
             pltpu.VMEM(by_line + (cut, width), bf16),
             pltpu.VMEM(by_line + (cut, width), bf16),
@@ -461,17 +497,14 @@
             pltpu.VMEM((FAR, unit, width), bf16),
             pltpu.VMEM((FAR, unit, width), bf16),
             pltpu.VMEM((unit, width), f32),
-            dma((2, 3)), dma((14,)), dma((2, FAR)), dma((2, 4)), dma((2, 2 * SIDE)), dma((2, 4 * SIDE)),
-            dma((2, 4)), dma((2, FAR)), dma((2, 4 * SIDE)), dma((2, 4 * SIDE)),
+            dma((2, 3)), dma((13,)), dma((2, FAR)), dma((2, 4)), dma((2, 2 * SIDE)), dma((2, 4 * SIDE)),
+            dma((2, 4)), dma((2, FAR)), dma((2, 4 * SIDE)), dma((2, 4 * SIDE)), dma((4,)),
         ],
-        compiler_params=pltpu.CompilerParams(collective_id=0, has_side_effects=True, vmem_limit_bytes=48 << 20),
+        compiler_params=pltpu.CompilerParams(collective_id=0, has_side_effects=True, vmem_limit_bytes=63400000),
         name="step",
-    )(send_counts.reshape(peers), piece, request_ids.reshape(by_owner + (1, capacity)),
+    )(send_counts.reshape(peers), table, request_ids.reshape(by_owner + (1, capacity)),
       entry_slots.T, entry_weights.T, pooled_grad)
 
-    pooled = lax.dot_general(
-        inc, arrived.reshape(slots, width), (((0,), (0,)), ((), ())), preferred_element_type=f32
-    ).astype(bf16)
     grad = grad.reshape(rows, width)
     fresh = accum + grad * grad
     return pooled, table - learn_rate * grad / jnp.sqrt(fresh), fresh

time: 144 us -> 140 us (0.972)
  local copies, waits for them, and re-layouts: 5.68 us -> 0.85 us
    unnamed x14 -> x7, local copies, waits for them, and re-layouts: 4.91 us -> 0.85 us
where the time goes in v3:
time: 140 us; the launch traced here: 139 us
  Pallas kernels  134 us (96%)
  other arithmetic  3.12 us (2%)
    pallas_call x1, Pallas kernels, per_device(): pl.pallas_call(functools.partial(step, n), in_specs=[pl.BlockSpec(memory_...  134 us

profile of v3, /device:TPU:1, one launch (start us, length us, event | category | flops | bytes accessed | tf_op | source)
XLA Modules:
  0.0 138.7 jit_solution(14512206753202130060)
XLA Ops:
  0.6 134.0 %step.1 = (bf16[256,128]{1,0:T(8,128)(2,1)}, f32[4,4,2,64,128]{4,3,2,1,0:T(8,128)}) custom-call(s32[32]{0:T(128)} %bitcast.14, f32[2048,128]{1,0:T(8,128)} %table_ref.1, s32[4,4,2,1,128]{4,3,2,1,0:T(1,128)} %bitcast.11, s32[16,256]{1,0:T(8,128)} %bitcast.12, bf16[16,256]{1,0:T(8,128)(2,1)} %bitcast.13, bf16[256,128]{1,0:T(8,128)(2,1)} %cot_hbm.1), custom_call_target="tpu_custom_call" | custom-call | tf_op jit(solution)/shard_map/step/pallas_call | solution.py:456
  134.7 0.0 copy-start
  134.7 0.0 copy-start.1
  134.7 1.6 %broadcast_multiply_fusion = (f32[4,4,2,64,128]{4,3,2,1,0:T(8,128)S(1)}, f32[4,4,2,64,128]{4,3,2,1,0:T(8,128)S(1)}) fusion(f32[4,4,2,64,128]{4,3,2,1,0:T(8,128)} %get-tuple-element.6), kind=kLoop, calls=%fused_computation.3 | loop fusion | flops 524288 | bytes 3145728 | tf_op jit(solution)/shard_map/mul | solution.py:510
  136.3 0.0 copy-done
  136.3 0.2 copy-done.1
  136.5 0.0 copy-start.2
  136.5 1.5 %fusion = (f32[2048,128]{1,0:T(8,128)}, f32[2048,128]{1,0:T(8,128)}) fusion(f32[2048,128]{1,0:T(8,128)S(1)} %copy-done, f32[4,4,2,64,128]{4,3,2,1,0:T(8,128)S(1)} %get-tuple-element.9, f32[2048,128]{1,0:T(8,128)S(1)} %copy-done.1, f32[4,4,2,64,128]{4,3,2,1,0:T(8,128)S(1)} %get-tuple-element.10), kind=kLoop, calls=%fused_computation.2 | loop fusion | flops 786432 | bytes 6291456 | tf_op jit(solution)/shard_map/sub | solution.py:510
  138.0 0.0 copy-done.2
  138.0 0.6 copy.11
Async XLA Ops:
  134.7 1.6 %copy-start = (f32[2048,128]{1,0:T(8,128)S(1)}, f32[2048,128]{1,0:T(8,128)}, u32[]{:S(2)}) copy-start(f32[2048,128]{1,0:T(8,128)} %table_ref.1) | copy-start | bytes 3145732
  134.7 1.8 %copy-start.1 = (f32[2048,128]{1,0:T(8,128)S(1)}, f32[2048,128]{1,0:T(8,128)}, u32[]{:S(2)}) copy-start(f32[2048,128]{1,0:T(8,128)} %param.8) | copy-start | bytes 3145732
  136.5 1.5 %copy-start.2 = (bf16[256,128]{1,0:T(8,128)(2,1)S(1)}, bf16[256,128]{1,0:T(8,128)(2,1)}, u32[]{:S(2)}) copy-start(bf16[256,128]{1,0:T(8,128)(2,1)} %get-tuple-element.14) | copy-start | bytes 196612

commit v4 on v3

--- a/solution.py
+++ b/solution.py
@@ -404,15 +404,19 @@
         far_sum = far_sum + far_in[o].astype(f32)
     piece[...] = far_sum
 
-    afar = grad_out.at[z // (2 * SIDE), lax.rem(z // 2, SIDE), lax.rem(z, 2)]
-    back_start, back_wait = seat.turn(piece, afar, grad_out.at[x, y, c], turn_sem.at[1])
-    back_start()
+    upper, lower = pl.ds(0, unit // 2), pl.ds(unit // 2, unit // 2)
+
+    def back(lines, k):
+        afar = grad_out.at[z // (2 * SIDE), lax.rem(z // 2, SIDE), lax.rem(z, 2), lines]
+        return seat.turn(piece.at[lines], afar, grad_out.at[x, y, c, lines], turn_sem.at[k])
+
+    upper_start, upper_wait = back(upper, 1)
+    lower_start, lower_wait = back(lower, 2)
+    upper_start()
+    lower_start()
     wait_own(11, 12)
     wait_each(SIDE, x_low_rows, y_high_rows)
     pool()
-    back_wait()
-
-    upper, lower = pl.ds(0, unit // 2), pl.ds(unit // 2, unit // 2)
 
     def share(ref, k, to):
         return remote(ref, ref, fin_sem.at[0, k], fin_sem.at[1, k], to, z)
@@ -429,13 +433,24 @@
     def x_lower(o):
         return share(grad_out.at[x, :, c, lower], 3 * SIDE + o, seat.along_x(o))
 
-    start_each(SIDE, x_upper, y_lower)
-    wait_each(SIDE, x_upper, y_lower)
-    start_each(SIDE, y_upper, x_lower)
-    wait_each(SIDE, y_upper, x_lower)
-    last = share(grad_out.at[:, :, c], 0, seat.twin)
-    last.start()
-    last.wait()
+    def twin_half(lines, k):
+        return share(grad_out.at[:, :, c, lines], k, seat.twin)
+
+    twins = twin_half(upper, 0), twin_half(lower, SIDE)
+    upper_wait()
+    start_each(SIDE, x_upper)
+    lower_wait()
+    start_each(SIDE, y_lower)
+    wait_each(SIDE, x_upper)
+    start_each(SIDE, y_upper)
+    wait_each(SIDE, y_lower)
+    start_each(SIDE, x_lower)
+    wait_each(SIDE, y_upper)
+    twins[0].start()
+    wait_each(SIDE, x_lower)
+    twins[1].start()
+    twins[0].wait()
+    twins[1].wait()
 
 
 def per_device(n, table, accum, request_ids, send_counts, entry_slots, entry_weights, pooled_grad):
@@ -497,7 +512,7 @@
             pltpu.VMEM((FAR, unit, width), bf16),
             pltpu.VMEM((FAR, unit, width), bf16),
             pltpu.VMEM((unit, width), f32),
-            dma((2, 3)), dma((13,)), dma((2, FAR)), dma((2, 4)), dma((2, 2 * SIDE)), dma((2, 4 * SIDE)),
+            dma((3, 3)), dma((13,)), dma((2, FAR)), dma((2, 4)), dma((2, 2 * SIDE)), dma((2, 4 * SIDE)),
             dma((2, 4)), dma((2, FAR)), dma((2, 4 * SIDE)), dma((2, 4 * SIDE)), dma((4,)),
         ],
         compiler_params=pltpu.CompilerParams(collective_id=0, has_side_effects=True, vmem_limit_bytes=63400000),

time: 140 us -> 140 us (level)
  no operation moved by 1% of the time
where the time goes in v4:
time: 140 us; the launch traced here: 139 us
  Pallas kernels  134 us (96%)
  other arithmetic  3.12 us (2%)
    pallas_call x1, Pallas kernels, per_device(): pl.pallas_call(functools.partial(step, n), in_specs=[pl.BlockSpec(memory_...  134 us

profile of v4, /device:TPU:1, one launch (start us, length us, event | category | flops | bytes accessed | tf_op | source)
XLA Modules:
  0.0 138.5 jit_solution(11537903038202288455)
XLA Ops:
  0.6 133.9 %step.1 = (bf16[256,128]{1,0:T(8,128)(2,1)}, f32[4,4,2,64,128]{4,3,2,1,0:T(8,128)}) custom-call(s32[32]{0:T(128)} %bitcast.14, f32[2048,128]{1,0:T(8,128)} %table_ref.1, s32[4,4,2,1,128]{4,3,2,1,0:T(1,128)} %bitcast.11, s32[16,256]{1,0:T(8,128)} %bitcast.12, bf16[16,256]{1,0:T(8,128)(2,1)} %bitcast.13, bf16[256,128]{1,0:T(8,128)(2,1)} %cot_hbm.1), custom_call_target="tpu_custom_call" | custom-call | tf_op jit(solution)/shard_map/step/pallas_call | solution.py:471
  134.5 0.0 copy-start
  134.5 0.0 copy-start.1
  134.5 1.6 %broadcast_multiply_fusion = (f32[4,4,2,64,128]{4,3,2,1,0:T(8,128)S(1)}, f32[4,4,2,64,128]{4,3,2,1,0:T(8,128)S(1)}) fusion(f32[4,4,2,64,128]{4,3,2,1,0:T(8,128)} %get-tuple-element.6), kind=kLoop, calls=%fused_computation.3 | loop fusion | flops 524288 | bytes 3145728 | tf_op jit(solution)/shard_map/mul | solution.py:525
  136.2 0.0 copy-done
  136.2 0.2 copy-done.1
  136.4 0.0 copy-start.2
  136.4 1.5 %fusion = (f32[2048,128]{1,0:T(8,128)}, f32[2048,128]{1,0:T(8,128)}) fusion(f32[2048,128]{1,0:T(8,128)S(1)} %copy-done, f32[4,4,2,64,128]{4,3,2,1,0:T(8,128)S(1)} %get-tuple-element.9, f32[2048,128]{1,0:T(8,128)S(1)} %copy-done.1, f32[4,4,2,64,128]{4,3,2,1,0:T(8,128)S(1)} %get-tuple-element.10), kind=kLoop, calls=%fused_computation.2 | loop fusion | flops 786432 | bytes 6291456 | tf_op jit(solution)/shard_map/sub | solution.py:525
  137.9 0.0 copy-done.2
  137.9 0.6 copy.11
Async XLA Ops:
  134.5 1.6 %copy-start = (f32[2048,128]{1,0:T(8,128)S(1)}, f32[2048,128]{1,0:T(8,128)}, u32[]{:S(2)}) copy-start(f32[2048,128]{1,0:T(8,128)} %table_ref.1) | copy-start | bytes 3145732
  134.5 1.8 %copy-start.1 = (f32[2048,128]{1,0:T(8,128)S(1)}, f32[2048,128]{1,0:T(8,128)}, u32[]{:S(2)}) copy-start(f32[2048,128]{1,0:T(8,128)} %param.8) | copy-start | bytes 3145732
  136.4 1.5 %copy-start.2 = (bf16[256,128]{1,0:T(8,128)(2,1)S(1)}, bf16[256,128]{1,0:T(8,128)(2,1)}, u32[]{:S(2)}) copy-start(bf16[256,128]{1,0:T(8,128)(2,1)} %get-tuple-element.14) | copy-start | bytes 196612
